TPU v7x, 32 devices: a whole 2x2x4 slice. The times are simulated.
32 devices in a mesh: dom: 2 (over y), orb: 16 (over z, x, core).
Axes of the slice: x: 2, y: 2, z: 4, core: 2. Of those that a mesh axis runs over, the one named last changes fastest.
Arguments:
- orbitals: float32 [2, 16, 64, 64, 128], P('dom', 'orb'), may hold values from -6 to 6
- occupations: float32 [2, 16], P('dom', 'orb'), may hold values from 0.01 to 0.2
- core_density: float32 [2, 64, 4096], P('dom'), may hold values from 0.1 to 2
- ion_potential: float32 [2, 64, 4096], P('dom'), may hold values from -3 to 3
- neighbors: int32 [2, 2], replicated, may hold values from 0 to 1, as said below
- margin_widths: int32 [2, 2], replicated, may hold values from 1 to 8, as said below
Outputs:
- orbitals_out: float32 [2, 16, 64, 64, 128], P('dom', 'orb')
- potential: float32 [2, 64, 4096], P('dom', None, 'orb')
Inputs may be any that keep to these rules, and one draw needn't show every extreme that they name: `neighbors`: each domain's left and right neighbours may be any domains, itself included, and two domains may share a neighbour. `margin_widths`: every draw has some entry equal to 8.
All inputs are finite; a program needn't handle non-finite values.
Results may differ from a plain program's by a relative error of at most 0.0001.
Values sent between devices are 32-bit elements; how exact they have to be, the bound alone decides.
A program may use at most 128 MiB of HBM per device.

v0:
```python
import math

import jax
import jax.numpy as jnp
from jax import lax
from jax.sharding import PartitionSpec as P

BUFFER = 8
STEPS = 2


EXCHANGE_COEF = (3.0 / math.pi) ** (1.0 / 3.0)
TIME_STEP = 0.5


def laplace(states):
    lead = [(0, 0)] * (states.ndim - 4)
    padded = jnp.pad(states, lead + [(1, 1), (1, 1), (0, 0), (1, 1)])
    summed = padded[..., 2:, 1:-1, :, 1:-1] + padded[..., :-2, 1:-1, :, 1:-1]
    summed = summed + padded[..., 1:-1, 2:, :, 1:-1] + padded[..., 1:-1, :-2, :, 1:-1]
    summed = summed + padded[..., 1:-1, 1:-1, :, 2:] + padded[..., 1:-1, 1:-1, :, :-2]
    return summed - 6.0 * states


def kinetic(states, half_step):
    result = states
    current = states
    for degree in range(1, 5):
        applied = -0.5 * laplace(current)
        factor = half_step / degree
        current = jnp.stack([factor * applied[..., 1, :], -factor * applied[..., 0, :]], axis=-2)
        result = result + current
    return result


def rotate_phase(states, potential_cube):
    rotation = TIME_STEP * potential_cube
    cosine = jnp.cos(rotation)
    sine_val = jnp.sin(rotation)
    real_part = states[..., 0, :]
    imag_part = states[..., 1, :]
    return jnp.stack(
        [cosine * real_part + sine_val * imag_part, cosine * imag_part - sine_val * real_part],
        axis=-2,
    )


def propagate(states, potential_cube):
    states = kinetic(states, 0.5 * TIME_STEP)
    states = rotate_phase(states, potential_cube)
    states = kinetic(states, 0.5 * TIME_STEP)
    return states


def mix_edges(lower_rows, upper_rows, from_left, from_right, own_widths):
    depth = lower_rows.shape[0]
    plane_pos = jnp.arange(depth).astype(jnp.float32)
    width_left = own_widths[0].astype(jnp.float32)
    width_right = own_widths[1].astype(jnp.float32)
    ramp_left = (jnp.maximum(width_left - plane_pos, 0.0) / (width_left + 1.0))[:, None]
    ramp_right = (jnp.maximum(plane_pos - (depth - width_right) + 1.0, 0.0) / (width_right + 1.0))[
        :, None
    ]
    mixed_lower = (1.0 - ramp_left) * lower_rows + ramp_left * from_left
    mixed_upper = (1.0 - ramp_right) * upper_rows + ramp_right * from_right
    return (mixed_lower, mixed_upper)


def trade_edges(lower_rows, upper_rows, neighbors, dom_index):
    stacked = jnp.stack([lower_rows, upper_rows])[None]
    gathered = lax.all_gather(stacked, "dom", axis=0, tiled=True)
    left_pack = lax.dynamic_index_in_dim(gathered, neighbors[dom_index, 0], 0, keepdims=False)
    right_pack = lax.dynamic_index_in_dim(gathered, neighbors[dom_index, 1], 0, keepdims=False)
    return (left_pack[1], right_pack[0])


def on_device(orbitals, occupations, core_density, ion_potential, neighbors, margin_widths):
    orbit_count = orbitals.shape[1]
    extent = orbitals.shape[2]
    states = orbitals.reshape(orbit_count, extent, extent, 2, extent)
    weights = occupations[0]
    dom_index = lax.axis_index("dom")
    own_widths = lax.dynamic_index_in_dim(margin_widths, dom_index, 0, keepdims=False)
    pieces = lax.axis_size("orb")
    columns = extent * extent // pieces
    first_col = lax.axis_index("orb") * columns
    core_full = core_density[0]
    ion_full = ion_potential[0]
    core_slab = lax.dynamic_slice_in_dim(core_full, first_col, columns, 1)
    ion_slab = lax.dynamic_slice_in_dim(ion_full, first_col, columns, 1)
    slab_potential = ion_slab
    for repeat in range(STEPS):
        squares = jnp.sum(states * states, axis=3)
        terms = jnp.sum(weights[:, None, None, None] * squares, axis=0).reshape(
            extent, extent * extent
        )
        density_slab = lax.psum_scatter(terms, "orb", scatter_dimension=1, tiled=True) + core_slab
        lower_rows = density_slab[:BUFFER]
        upper_rows = density_slab[extent - BUFFER :]
        from_left, from_right = trade_edges(lower_rows, upper_rows, neighbors, dom_index)
        mixed_lower, mixed_upper = mix_edges(
            lower_rows, upper_rows, from_left, from_right, own_widths
        )
        blended = jnp.concatenate(
            [mixed_lower, density_slab[BUFFER : extent - BUFFER], mixed_upper], axis=0
        )
        slab_potential = ion_slab - EXCHANGE_COEF * jnp.cbrt(blended)
        potential_full = lax.all_gather(slab_potential, "orb", axis=1, tiled=True)
        states = propagate(states, potential_full.reshape(extent, extent, extent))
    return (states.reshape(orbitals.shape), slab_potential[None])


def solution(mesh):
    return jax.shard_map(
        on_device,
        mesh=mesh,
        in_specs=(
            P("dom", "orb", None, None, None),
            P("dom", "orb"),
            P("dom", None, None),
            P("dom", None, None),
            P(),
            P(),
        ),
        out_specs=(P("dom", "orb", None, None, None), P("dom", None, "orb")),
        check_vma=False,
    )
```

profile of v0, /device:TPU:0, one launch (start us, length us, event | category | flops | bytes accessed | tf_op | source)
XLA Modules:
  0.0 361.9 jit_solution(13410099119543475300)
XLA Ops:
  7.2 5.6 %reshape.1412 = f32[1,64,64,2,64]{4,3,2,1,0:T(2,128)} reshape(f32[1,1,64,64,128]{4,3,2,1,0:T(8,128)} %param.6) | data formatting | bytes 4194304 | tf_op jit(solution)/shard_map/reshape | solution.py:80
  12.8 8.4 %multiply_reduce_fusion.1 = f32[64,64,64]{2,1,0:T(8,128)S(1)} fusion(f32[1,64,64,2,64]{4,3,2,1,0:T(2,128)} %reshape.1412), kind=kLoop, calls=%fused_computation.227 | loop fusion | flops 786432 | bytes 3145728 | tf_op jit(solution)/shard_map/reduce_sum | solution.py:93
  22.1 1.6 mul.632
  26.9 4.8 %copy.14 = f32[1,64,64,2,64]{4,2,1,3,0:T(8,128)} copy(f32[1,64,64,2,64]{4,3,2,1,0:T(2,128)} %reshape.1412) | data formatting | bytes 4194304 | tf_op jit(solution)/shard_map/reshape | solution.py:80
  33.5 13.5 %fusion.6 = f32[1,64,64,2,64]{4,2,1,3,0:T(8,128)S(1)} fusion(f32[1,64,64,2,64]{4,2,1,3,0:T(8,128)} %copy.14), kind=kLoop, calls=%fused_computation.102 | loop fusion | flops 4194304 | bytes 4194304 | tf_op jit(solution)/shard_map/mul | solution.py:29
  47.0 1.8 slice_multiply_fusion.31
  50.0 2.1 pad_maximum_fusion
  52.1 3.4 fusion.13
  56.1 1.3 copy-done.11
  58.5 4.8 %fusion.20 = f32[1,64,64,2,64]{4,2,1,3,0:T(8,128)} fusion(f32[1,64,64,2,64]{4,2,1,3,0:T(8,128)S(1)} %pad_maximum_fusion.1), kind=kLoop, calls=%fused_computation.116 | loop fusion | flops 4194304 | bytes 4194304 | tf_op jit(solution)/shard_map/mul | solution.py:29
  63.3 20.6 %reduce-scatter.3.cloned.1.call-done = f32[64,256]{1,0:T(8,128)} async-done(((f32[64,4096]{1,0:T(8,128)}), f32[64,256]{1,0:T(8,128)}) %reduce-scatter.3.cloned.1.call-update) | async-done | bytes 65552 | tf_op jit(solution)/shard_map/reduce_scatter | solution.py:97
  83.9 0.9 bitcast_add_fusion.1
  84.8 4.4 %all-gather = f32[4,8,256]{2,1,0:T(8,128)S(1)} all-gather(f32[2,8,256]{2,1,0:T(8,128)S(1)} %pad_maximum_fusion.14), channel_id=2, replica_groups=mesh['dom'=2,'orb'=16] {'dom'}, dimensions={0}, use_global_device_ids=true | all-gather | bytes 49152 | tf_op jit(solution)/shard_map/all_gather | solution.py:71
  89.3 1.5 fusion.113
  90.9 2.7 slice_multiply_fusion.27
  94.5 5.0 %fusion.27 = f32[1,64,64,2,64]{4,2,1,3,0:T(8,128)} fusion(f32[1,64,64,2,64]{4,2,1,3,0:T(8,128)S(1)} %pad_maximum_fusion.2), kind=kLoop, calls=%fused_computation.123 | loop fusion | flops 4194304 | bytes 4194304 | tf_op jit(solution)/shard_map/mul | solution.py:29
  99.5 2.8 slice_multiply_fusion.25
  104.3 3.6 maximum_add_fusion
  107.8 19.1 %all-gather.5.cloned.1.call-done = f32[64,4096]{1,0:T(8,128)} async-done(((f32[64,256]{1,0:T(8,128)}), f32[64,4096]{1,0:T(8,128)}) %all-gather.5.cloned.1.call-update) | async-done | bytes 1048592 | tf_op jit(solution)/shard_map/all_gather | solution.py:108
  126.9 5.5 %multiply_cosine_fusion.1 = (f32[64,4096]{1,0:T(8,128)}, f32[64,4096]{1,0:T(8,128)S(1)}) fusion(f32[64,4096]{1,0:T(8,128)} %all-gather.5.cloned.1.call-done), kind=kLoop, calls=%fused_computation.269 | loop fusion | flops 262144 | bytes 3145728 | tf_op jit(solution)/shard_map/cos | solution.py:38
  132.4 2.0 cos.33
  134.4 2.2 sin.33
  136.6 3.9 %multiply_add_fusion.1 = (f32[1,64,64,1,64]{4,2,1,3,0:T(8,128)S(1)}, f32[1,64,64,1,64]{4,2,1,3,0:T(8,128)S(1)}) fusion(f32[1,64,64,1,64]{4,2,1,3,0:T(8,128)} %sin.33, f32[1,64,64,1,64]{4,2,1,3,0:T(8,128)S(1)} %cos.33, f32[1,64,64,2,64]{4,2,1,3,0:T(8,128)} %maximum_add_fusion), kind=kLoop, calls=%fused_computation.263 | loop fusion | flops 1572864 | bytes 6291456 | tf_op jit(solution)/shard_map/add | solution.py:43
  141.3 3.4 fusion.34
  144.7 0.8 slice_multiply_fusion.23
  146.4 3.4 fusion.41
  149.9 0.8 slice_multiply_fusion.21
  151.5 5.2 %fusion.48 = f32[1,64,64,2,64]{4,2,1,3,0:T(8,128)} fusion(f32[1,64,64,2,64]{4,2,1,3,0:T(8,128)S(1)} %pad_maximum_fusion.5), kind=kLoop, calls=%fused_computation.144 | loop fusion | flops 4194304 | bytes 4194304 | tf_op jit(solution)/shard_map/mul | solution.py:29
  156.7 2.7 slice_multiply_fusion.19
  159.4 2.4 pad_maximum_fusion.6
  161.8 14.8 %fusion.55 = f32[1,64,64,2,64]{4,2,1,3,0:T(8,128)} fusion(f32[1,64,64,2,64]{4,2,1,3,0:T(8,128)} %pad_maximum_fusion.6), kind=kLoop, calls=%fused_computation.151 | loop fusion | flops 4194304 | bytes 4194304 | tf_op jit(solution)/shard_map/mul | solution.py:29
  176.6 2.7 slice_multiply_fusion.17
  179.3 4.4 %multiply_reduce_fusion = (f32[64,64,64]{2,1,0:T(8,128)S(1)}, f32[1,64,64,2,64]{4,2,1,3,0:T(8,128)}) fusion(f32[1,64,64,1,64]{4,2,1,3,0:T(8,128)S(1)} %get-tuple-element.29, f32[1,64,64,1,64]{4,2,1,3,0:T(8,128)S(1)} %get-tuple-element.28, f32[1,64,64,1,64]{4,2,1,3,0:T(8,128)S(1)} %get-tuple-element.31, f32[1,64,64,1,64]{4,2,1,3,0:T(8,128)S(1)} %get-tuple-element.30, ...), kind=kLoop, calls=%fused_computation.226 | loop fusion | flops 5505024 | bytes 13631488 | tf_op jit(solution)/shard_map/reduce_sum | solution.py:93
  183.9 1.6 mul.680
  185.6 13.4 %fusion.62 = f32[1,64,64,2,64]{4,2,1,3,0:T(8,128)S(1)} fusion(f32[1,64,64,2,64]{4,2,1,3,0:T(8,128)} %get-tuple-element.3), kind=kLoop, calls=%fused_computation.158 | loop fusion | flops 4194304 | bytes 4194304 | tf_op jit(solution)/shard_map/mul | solution.py:29
  199.5 1.4 copy-done.5
  201.3 3.4 fusion.69
  205.2 1.3 copy-done.7
  207.7 4.8 %fusion.76 = f32[1,64,64,2,64]{4,2,1,3,0:T(8,128)} fusion(f32[1,64,64,2,64]{4,2,1,3,0:T(8,128)S(1)} %pad_maximum_fusion.8), kind=kLoop, calls=%fused_computation.172 | loop fusion | flops 4194304 | bytes 4194304 | tf_op jit(solution)/shard_map/mul | solution.py:29
  212.5 30.2 %reduce-scatter.5.cloned.1.call-done = f32[64,256]{1,0:T(8,128)} async-done(((f32[64,4096]{1,0:T(8,128)}), f32[64,256]{1,0:T(8,128)}) %reduce-scatter.5.cloned.1.call-update) | async-done | bytes 65552 | tf_op jit(solution)/shard_map/reduce_scatter | solution.py:97
  242.6 0.9 bitcast_add_fusion
  243.5 4.4 %all-gather.1 = f32[4,8,256]{2,1,0:T(8,128)S(1)} all-gather(f32[2,8,256]{2,1,0:T(8,128)S(1)} %pad_maximum_fusion.15), channel_id=3, replica_groups=mesh['dom'=2,'orb'=16] {'dom'}, dimensions={0}, use_global_device_ids=true | all-gather | bytes 49152 | tf_op jit(solution)/shard_map/all_gather | solution.py:71
  248.0 1.5 fusion.115
  249.6 2.7 slice_multiply_fusion.11
  253.1 5.0 %fusion.83 = f32[1,64,64,2,64]{4,2,1,3,0:T(8,128)} fusion(f32[1,64,64,2,64]{4,2,1,3,0:T(8,128)S(1)} %pad_maximum_fusion.9), kind=kLoop, calls=%fused_computation.179 | loop fusion | flops 4194304 | bytes 4194304 | tf_op jit(solution)/shard_map/mul | solution.py:29
  258.1 2.8 slice_multiply_fusion.9
  262.9 3.9 %maximum_add_fusion.2 = f32[1,64,64,2,64]{4,2,1,3,0:T(8,128)} fusion(f32[1,64,64,1,64]{4,2,1,3,0:T(8,128)S(1)} %get-tuple-element.21, f32[1,64,64,1,64]{4,2,1,3,0:T(8,128)S(1)} %get-tuple-element.20, f32[1,64,64,2,64]{4,2,1,3,0:T(8,128)S(1)} %copy-done.3, f32[1,64,64,1,64]{4,2,1,3,0:T(8,128)S(1)} %get-tuple-element.23, ...), kind=kLoop, calls=%fused_computation.220 | loop fusion | flops 4194304 | bytes 12582912 | tf_op jit(solution)/shard_map/add | solution.py:32
  266.7 1.5 fusion.117
  268.3 17.3 %all-gather.7.cloned.1.call-done = f32[64,4096]{1,0:T(8,128)} async-done(((f32[64,256]{1,0:T(8,128)}), f32[64,4096]{1,0:T(8,128)}) %all-gather.7.cloned.1.call-update) | async-done | bytes 1048592 | tf_op jit(solution)/shard_map/all_gather | solution.py:108
  285.6 5.5 %multiply_cosine_fusion = (f32[64,4096]{1,0:T(8,128)}, f32[64,4096]{1,0:T(8,128)S(1)}) fusion(f32[64,4096]{1,0:T(8,128)} %all-gather.7.cloned.1.call-done), kind=kLoop, calls=%fused_computation.267 | loop fusion | flops 262144 | bytes 3145728 | tf_op jit(solution)/shard_map/cos | solution.py:38
  291.1 2.0 cos.35
  293.1 2.2 sin.35
  295.2 3.9 %multiply_add_fusion = (f32[1,64,64,1,64]{4,2,1,3,0:T(8,128)S(1)}, f32[1,64,64,1,64]{4,2,1,3,0:T(8,128)S(1)}) fusion(f32[1,64,64,1,64]{4,2,1,3,0:T(8,128)} %sin.35, f32[1,64,64,1,64]{4,2,1,3,0:T(8,128)S(1)} %cos.35, f32[1,64,64,2,64]{4,2,1,3,0:T(8,128)} %maximum_add_fusion.2), kind=kLoop, calls=%fused_computation.261 | loop fusion | flops 1572864 | bytes 6291456 | tf_op jit(solution)/shard_map/add | solution.py:43
  299.9 3.4 fusion.90
  303.4 0.8 slice_multiply_fusion.7
  305.0 3.7 %fusion.97 = f32[1,64,64,2,64]{4,2,1,3,0:T(8,128)S(1)} fusion(f32[1,64,64,2,64]{4,2,1,3,0:T(8,128)S(1)} %pad_maximum_fusion.11), kind=kLoop, calls=%fused_computation.193 | loop fusion | flops 4194304 | bytes 4194304 | tf_op jit(solution)/shard_map/mul | solution.py:29
  310.4 4.7 %fusion.104 = f32[1,64,64,2,64]{4,2,1,3,0:T(8,128)} fusion(f32[1,64,64,2,64]{4,2,1,3,0:T(8,128)S(1)} %pad_maximum_fusion.12), kind=kLoop, calls=%fused_computation.200 | loop fusion | flops 4194304 | bytes 4194304 | tf_op jit(solution)/shard_map/mul | solution.py:29
  315.1 2.7 slice_multiply_fusion.3
  317.8 2.4 pad_maximum_fusion.13
  320.2 14.8 %fusion.111 = f32[1,64,64,2,64]{4,2,1,3,0:T(8,128)} fusion(f32[1,64,64,2,64]{4,2,1,3,0:T(8,128)} %pad_maximum_fusion.13), kind=kLoop, calls=%fused_computation.207 | loop fusion | flops 4194304 | bytes 4194304 | tf_op jit(solution)/shard_map/mul | solution.py:29
  335.0 2.7 slice_multiply_fusion.1
  337.7 4.0 %maximum_add_fusion.3 = f32[1,64,64,2,64]{4,2,1,3,0:T(8,128)} fusion(f32[1,64,64,1,64]{4,2,1,3,0:T(8,128)S(1)} %get-tuple-element.13, f32[1,64,64,1,64]{4,2,1,3,0:T(8,128)S(1)} %get-tuple-element.12, f32[1,64,64,1,64]{4,2,1,3,0:T(8,128)S(1)} %get-tuple-element.15, f32[1,64,64,1,64]{4,2,1,3,0:T(8,128)S(1)} %get-tuple-element.14, ...), kind=kLoop, calls=%fused_computation.225 | loop fusion | flops 4718592 | bytes 12582912 | tf_op jit(solution)/shard_map/add | solution.py:32
  341.6 8.1 %copy.15 = f32[1,64,64,2,64]{4,3,2,1,0:T(2,128)} copy(f32[1,64,64,2,64]{4,2,1,3,0:T(8,128)} %maximum_add_fusion.3) | data formatting | bytes 4194304 | tf_op jit(solution)/shard_map/add | solution.py:32
  349.7 5.4 %add.695 = f32[1,1,64,64,128]{4,3,2,1,0:T(8,128)} reshape(f32[1,64,64,2,64]{4,3,2,1,0:T(2,128)} %copy.15) | data formatting | bytes 4194304 | tf_op jit(solution)/shard_map/add | solution.py:32
  (66 shorter events, 17.3 us)
Async XLA Ops:
  7.2 24.5 %copy-start = (s32[2,2]{1,0:T(2,128)S(1)}, s32[2,2]{1,0:T(2,128)}, u32[]{:S(2)}) copy-start(s32[2,2]{1,0:T(2,128)} %param.11) | copy-start | bytes 52
  7.2 76.7 %reduce-scatter.3.cloned.1.call-start = ((), (), s32[]{:S(2)}) async-start(), calls=%async_computation.2 | async-start | bytes 1114112 | tf_op jit(solution)/shard_map/reduce_scatter | solution.py:97
  21.9 2.1 copy-start.15
  23.7 103.2 %all-gather.5.cloned.1.call-start = ((), (), s32[]{:S(2)}) async-start(), calls=%async_computation.3 | async-start | bytes 1114112 | tf_op jit(solution)/shard_map/all_gather | solution.py:108
  56.0 1.3 copy-start.11
  56.1 2.0 copy-start.13
  90.9 151.7 %reduce-scatter.5.cloned.1.call-start = ((), (), s32[]{:S(2)}) async-start(), calls=%async_computation.4 | async-start | bytes 1114112 | tf_op jit(solution)/shard_map/reduce_scatter | solution.py:97
  94.5 7.9 %copy-start.14 = (f32[1,64,64,1,64]{4,2,1,3,0:T(8,128)S(1)}, f32[1,64,64,1,64]{4,2,1,3,0:T(8,128)}, u32[]{:S(2)}) copy-start(f32[1,64,64,1,64]{4,2,1,3,0:T(8,128)} %copy-done.13) | copy-start | bytes 3145732
  99.5 3.5 copy-start.2
  99.5 4.1 %copy-start.4 = (f32[1,64,64,1,64]{4,2,1,3,0:T(8,128)S(1)}, f32[1,64,64,1,64]{4,2,1,3,0:T(8,128)}, u32[]{:S(2)}) copy-start(f32[1,64,64,1,64]{4,2,1,3,0:T(8,128)} %get-tuple-element.43) | copy-start | bytes 3145732
  99.5 4.7 %copy-start.12 = (f32[1,64,64,1,64]{4,2,1,3,0:T(8,128)S(1)}, f32[1,64,64,1,64]{4,2,1,3,0:T(8,128)}, u32[]{:S(2)}) copy-start(f32[1,64,64,1,64]{4,2,1,3,0:T(8,128)} %copy-done.11) | copy-start | bytes 3145732
  185.6 100.0 %all-gather.7.cloned.1.call-start = ((), (), s32[]{:S(2)}) async-start(), calls=%async_computation.5 | async-start | bytes 1114112 | tf_op jit(solution)/shard_map/all_gather | solution.py:108
  199.5 1.4 copy-start.5
  205.2 1.3 copy-start.7
  205.2 2.0 copy-start.9
  253.1 7.8 %copy-start.10 = (f32[1,64,64,1,64]{4,2,1,3,0:T(8,128)S(1)}, f32[1,64,64,1,64]{4,2,1,3,0:T(8,128)}, u32[]{:S(2)}) copy-start(f32[1,64,64,1,64]{4,2,1,3,0:T(8,128)} %copy-done.9) | copy-start | bytes 3145732
  258.1 3.5 copy-start.3
  258.1 4.1 %copy-start.6 = (f32[1,64,64,1,64]{4,2,1,3,0:T(8,128)S(1)}, f32[1,64,64,1,64]{4,2,1,3,0:T(8,128)}, u32[]{:S(2)}) copy-start(f32[1,64,64,1,64]{4,2,1,3,0:T(8,128)} %copy-done.5) | copy-start | bytes 3145732
  258.1 4.7 %copy-start.8 = (f32[1,64,64,1,64]{4,2,1,3,0:T(8,128)S(1)}, f32[1,64,64,1,64]{4,2,1,3,0:T(8,128)}, u32[]{:S(2)}) copy-start(f32[1,64,64,1,64]{4,2,1,3,0:T(8,128)} %copy-done.7) | copy-start | bytes 3145732
  341.6 13.5 %copy-start.1 = (s32[2,2]{1,0:T(2,128)S(1)}, s32[2,2]{1,0:T(2,128)}, u32[]{:S(2)}) copy-start(s32[2,2]{1,0:T(2,128)} %param.11) | copy-start | bytes 52
Sparse Core Ops, SparseCore 0:
  23.9 60.0 reduce-scatter.2
  91.0 35.8 all-gather.4
  185.7 56.8 reduce-scatter.4
  249.7 35.8 all-gather.6
where the time goes:
time: 369 us; the launch traced here: 362 us
  other arithmetic  200 us (54%)
  waiting for transfers between devices  87.3 us (24%)
  local copies, waits for them, and re-layouts  45.9 us (12%)
  between operations  20 us (5%)
  blocking collectives  8.83 us (2%)
    mul x16, other arithmetic, kinetic(): applied = -0.5 * laplace(current)  107 us
    reduce_scatter x2, waiting for transfers between devices, on_device(): lax.psum_scatter(terms, 'orb', scatter_dimension=1, tiled=True) + core_slab  50.8 us
    all_gather x2, waiting for transfers between devices, on_device(): potential_full = lax.all_gather(slab_potential, 'orb', axis=1, tiled=True)  36.4 us
    mul x16, other arithmetic, kinetic(): factor * applied[..., 1, :]  28.2 us
    add x2, local copies, waits for them, and re-layouts, kinetic(): result = result + current  13.5 us
    another operation x12, other arithmetic, kinetic(): jnp.stack([factor * applied[..., 1, :], -factor * applied[..., 0, :]], ax...  13.1 us
    reduce_sum x2, other arithmetic, on_device(): squares = jnp.sum(states * states, axis=3)  12.8 us
    add x3, other arithmetic, kinetic(): result = result + current  11.4 us
  transfers between devices with their start and end apart: 4, of which 4 were waited for; matrix products, arithmetic and copies ran while one was open for 24% of the time, Pallas kernels for 0%

commit v1 on v0

v1 whole, which is shorter than its diff:
```python
import functools
import math

import jax
import jax.numpy as jnp
from jax import lax
from jax.experimental import pallas as pl
from jax.experimental.pallas import tpu as pltpu
from jax.sharding import PartitionSpec as P

BUFFER = 8
STEPS = 2
CHUNKS = 4
GRID = 64
LANES = 128
EXCHANGE_COEF = (3.0 / math.pi) ** (1.0 / 3.0)
H = 0.125
MESH = pl.DeviceIdType.MESH


def kernel(
    n, doms,
    orb_ref, occ_ref, nbr_ref, wid_ref, core_hbm, ion_hbm,
    out_ref, pot_ref,
    psi, u1, u2, u3, core_v, ion_v,
    dens, vbuf, recv_a, recv_b, recv_c, edges_0, edges_1,
    load_sem,
    a_send, a_recv, b_send, b_recv, c_send, c_recv,
    d_send, d_recv, z_send, z_recv, x_send, x_recv, k_send, k_recv,
):
    half = n // 2
    far = n // 4
    r = GRID * GRID // (LANES * n)
    planes = GRID // CHUNKS
    rows = planes * r
    dom = lax.axis_index("dom")
    p = lax.axis_index("orb")
    c = lax.rem(p, 2)
    b = lax.rem(p // 2, 2)
    a = p // 4
    m = p // 2
    core_peer = p + 1 - 2 * c
    x_peer = p + 2 - 4 * b

    def z_peer(i):
        other = lax.rem(a + i, far)
        return other, other * 4 + b * 2 + c

    def d_peer(i):
        return lax.rem(dom + i, doms)

    barrier = pltpu.get_barrier_semaphore()
    peers = [(dom, core_peer), (dom, x_peer)]
    peers += [(dom, z_peer(i)[1]) for i in range(1, far)]
    peers += [(d_peer(i), p) for i in range(1, doms)]
    for peer in peers:
        pl.semaphore_signal(barrier, inc=1, device_id=peer, device_id_type=MESH)

    first_col = pl.multiple_of(p * (r * LANES), LANES)
    loads = [
        pltpu.make_async_copy(core_hbm.at[:, pl.ds(first_col, r * LANES)], core_v, load_sem.at[0]),
        pltpu.make_async_copy(ion_hbm.at[:, pl.ds(first_col, r * LANES)], ion_v, load_sem.at[1]),
    ]
    for load in loads:
        load.start()

    weight = occ_ref[0, 0]
    lane = lax.broadcasted_iota(jnp.int32, (8, LANES), 1)
    low = lane < GRID
    sign = jnp.where(low, 1.0, -1.0)
    z_first = jnp.bitwise_and(lane, GRID - 1) == 0
    z_last = jnp.bitwise_and(lane, GRID - 1) == GRID - 1
    sub = lax.broadcasted_iota(jnp.int32, (8, LANES), 0)

    def rows_at(k, core, mm):
        return pl.multiple_of(((k * 2 + core) * half + mm) * rows, 8)

    def column_start(x, jj):
        k = x // planes
        xr = x - k * planes
        core = (jj // r) % 2
        extra = jj // (2 * r)
        return ((k * 2 + core) * half + extra) * rows + xr * r + jj % r

    stride = (4 // (2 * r)) * rows

    def put_density(x, plane):
        total = []
        for j in range(8):
            sq = plane[j] * plane[j]
            total.append(weight * (sq + pltpu.roll(sq, GRID, 1)))
        for jj in range(4):
            packed = jnp.where(low, total[2 * jj], total[2 * jj + 1])
            dens[pl.ds(column_start(x, jj), 8, stride=stride), :] = packed

    def stencil(src, x):
        mid = [src[x + 1, j] for j in range(8)]
        before_edge = jnp.where(sub == 0, 0.0, pltpu.roll(mid[7], 1, 0))
        after_edge = jnp.where(sub == 7, 0.0, pltpu.roll(mid[0], 7, 0))
        res = []
        for j in range(8):
            total = src[x, j] + src[x + 2, j]
            total += (mid[j - 1] if j else before_edge) + (mid[j + 1] if j < 7 else after_edge)
            total += jnp.where(z_first, 0.0, pltpu.roll(mid[j], 1, 1))
            total += jnp.where(z_last, 0.0, pltpu.roll(mid[j], LANES - 1, 1))
            res.append(6.0 * mid[j] - total)
        return res, mid

    def loop(start, stop, body, unroll=2):
        def step(i, carry):
            for o in range(unroll):
                body(start + i * unroll + o)
            return carry
        lax.fori_loop(0, (stop - start) // unroll, step, 0)

    def sweep(src, dst):
        def body(x):
            res, _ = stencil(src, x)
            for j in range(8):
                dst[x + 1, j] = res[j]
        loop(0, GRID, body)

    def last_sweep(emit):
        def body(x):
            res, mid = stencil(u3, x)
            plane = []
            for j in range(8):
                odd = H * u1[x + 1, j] - (H**3 / 6) * mid[j]
                even = psi[x + 1, j] - (H**2 / 2) * u2[x + 1, j] + (H**4 / 24) * res[j]
                plane.append(even + sign * pltpu.roll(odd, GRID, 1))
            emit(x, plane)
        return body

    def keep(x, plane):
        for j in range(8):
            psi[x + 1, j] = plane[j]

    def finish(x, plane):
        for j in range(8):
            out_ref[x, pl.ds(j, 8, stride=8), :] = plane[j]

    def phase(t):
        def body(x):
            for jj in range(4):
                v = vbuf[t, pl.ds(column_start(x, jj), 8, stride=stride), :]
                turns = jnp.floor(v * (0.25 / math.pi) + 0.5)
                ang = (v * 0.25 - turns * 3.140625) - turns * (math.pi - 3.140625)
                q = ang * ang
                s = ang * (1.0 + q * (-1 / 6 + q * (1 / 120 + q * (-1 / 5040 + q * (1 / 362880 - q / 39916800)))))
                co = 1.0 + q * (-0.5 + q * (1 / 24 + q * (-1 / 720 + q * (1 / 40320 + q * (-1 / 3628800 + q / 479001600)))))
                sin = 2.0 * s * co
                cos = 1.0 - 2.0 * s * s
                sin_r = pltpu.roll(sin, GRID, 1)
                cos_r = pltpu.roll(cos, GRID, 1)
                for o in range(2):
                    cc = jnp.where(low, cos_r, cos) if o else jnp.where(low, cos, cos_r)
                    ss = jnp.where(low, sin_r, -sin) if o else jnp.where(low, sin, -sin_r)
                    f = psi[x + 1, 2 * jj + o]
                    psi[x + 1, 2 * jj + o] = cc * f + ss * pltpu.roll(f, GRID, 1)
        return body

    zero = jnp.zeros((8, 8, LANES), jnp.float32)
    for ref in (psi, u1, u2, u3):
        ref[0] = zero
        ref[GRID + 1] = zero

    def remote(src, dst, send, recv, peer):
        return pltpu.make_async_remote_copy(
            src_ref=src, dst_ref=dst, send_sem=send, recv_sem=recv,
            device_id=peer, device_id_type=MESH,
        )

    def load_in(x):
        plane = [orb_ref[x, pl.ds(j, 8, stride=8), :] for j in range(8)]
        keep(x, plane)
        put_density(x, plane)

    def density_again(x):
        put_density(x, [psi[x + 1, j] for j in range(8)])

    order = [1, 2, 0, 3] if CHUNKS == 4 else list(range(CHUNKS))
    order = [k for k in (0, CHUNKS - 1)] + [k for k in range(1, CHUNKS - 1)]
    for t in range(STEPS):
        edges = (edges_0, edges_1)[t]
        sends = []

        def go(copy):
            copy.start()
            sends.append(copy)
            return copy

        a_copies = {}
        for k in order:
            loop(k * planes, (k + 1) * planes, density_again if t else load_in)
            if t == 0 and k == order[0]:
                pl.semaphore_wait(barrier, len(peers))
            a_copies[k] = go(remote(
                dens.at[pl.ds(rows_at(k, 1 - c, 0), half * rows)],
                recv_a.at[t, k], a_send.at[t, k], a_recv.at[t, k], (dom, core_peer)))
        sweep(psi, u1)
        b_copies = {}
        for k in order:
            a_copies[k].wait_recv()
            for mm in range(half):
                at = pl.ds(rows_at(k, c, mm), rows)
                dens[at, :] = dens[at, :] + recv_a[t, k, pl.ds(mm * rows, rows), :]
            b_copies[k] = []
            for i in range(far):
                b_copies[k].append(go(remote(
                    dens.at[pl.ds(rows_at(k, c, 2 * i + 1 - b), rows)],
                    recv_b.at[t, k, i], b_send.at[t, k, i], b_recv.at[t, k, i], (dom, x_peer))))
        sweep(u1, u2)
        c_copies = {}
        for k in order:
            for i in range(far):
                b_copies[k][i].wait_recv()
                at = pl.ds(rows_at(k, c, 2 * i + b), rows)
                dens[at, :] = dens[at, :] + recv_b[t, k, i]
            c_copies[k] = []
            for i in range(1, far):
                other, peer = z_peer(i)
                c_copies[k].append(go(remote(
                    dens.at[pl.ds(rows_at(k, c, 2 * other + b), rows)],
                    recv_c.at[t, k, i - 1], c_send.at[t, k, i - 1], c_recv.at[t, k, i - 1], (dom, peer))))
        sweep(u2, u3)
        if t == 0:
            for load in loads:
                load.wait()

        def total_density(k):
            for copy in c_copies[k]:
                copy.wait_recv()
            base = rows_at(k, c, m)
            at = pl.ds(base, rows)
            total = dens[at, :]
            for i in range(far - 1):
                total = total + recv_c[t, k, i]
            dens[at, :] = total
            parts = []
            for rr in range(r):
                parts.append(
                    dens[pl.ds(base + rr, planes, stride=r), :]
                    + core_v[k * planes:(k + 1) * planes, rr * LANES:(rr + 1) * LANES])
            return parts

        z_copies = {}

        def put_potential(k, parts):
            base = rows_at(k, c, m)
            for rr in range(r):
                cols = slice(rr * LANES, (rr + 1) * LANES)
                span = slice(k * planes, (k + 1) * planes)
                root = jnp.exp(jnp.log(parts[rr]) * (1.0 / 3.0))
                root = root - (root - parts[rr] / (root * root)) * (1.0 / 3.0)
                v = ion_v[span, cols] - EXCHANGE_COEF * root
                vbuf[t, pl.ds(base + rr, planes, stride=r), :] = v
                if t == STEPS - 1:
                    pot_ref[span, cols] = v
            z_copies[k] = []
            for i in range(1, far):
                at = pl.ds(base, rows)
                z_copies[k].append(go(remote(
                    vbuf.at[t, at], vbuf.at[t, at],
                    z_send.at[t, k, i - 1], z_recv.at[t, k, i - 1], (dom, z_peer(i)[1]))))

        kept = {}
        for side, k in ((0, 0), (1, CHUNKS - 1)):
            kept[k] = total_density(k)
            span = slice(0, 8) if side == 0 else slice(planes - 8, planes)
            for rr in range(r):
                edges[dom, side, rr] = kept[k][rr][span]
        d_copies = [
            go(remote(edges.at[dom], edges.at[dom],
                      d_send.at[t, i - 1], d_recv.at[t, i - 1], (d_peer(i), p)))
            for i in range(1, doms)
        ]
        for k in range(1, CHUNKS - 1):
            put_potential(k, total_density(k))
        for copy in d_copies:
            copy.wait_recv()
        pos = sub.astype(jnp.float32)
        for side, k in ((0, 0), (1, CHUNKS - 1)):
            width = wid_ref[dom, side].astype(jnp.float32)
            source = nbr_ref[dom, side]
            if side == 0:
                ramp = jnp.maximum(width - pos, 0.0) / (width + 1.0)
            else:
                ramp = jnp.maximum(pos - (BUFFER - width) + 1.0, 0.0) / (width + 1.0)
            parts = []
            for rr in range(r):
                rho = kept[k][rr]
                own = rho[:8] if side == 0 else rho[planes - 8:]
                mixed = (1.0 - ramp) * own + ramp * edges[source, 1 - side, rr]
                both = [mixed, rho[8:]] if side == 0 else [rho[:planes - 8], mixed]
                parts.append(jnp.concatenate(both, axis=0))
            put_potential(k, parts)

        loop(0, GRID, last_sweep(keep))
        back = [k for k in range(1, CHUNKS - 1)] + [0, CHUNKS - 1]
        x_copies = {}
        for k in back:
            x_copies[k] = []
            for i in range(far):
                if i:
                    z_copies[k][i - 1].wait_recv()
                owner = lax.rem(a + far - i, far)
                at = pl.ds(rows_at(k, c, 2 * owner + b), rows)
                x_copies[k].append(go(remote(
                    vbuf.at[t, at], vbuf.at[t, at],
                    x_send.at[t, k, i], x_recv.at[t, k, i], (dom, x_peer))))
        k_copies = {}
        for k in back:
            for copy in x_copies[k]:
                copy.wait_recv()
            at = pl.ds(rows_at(k, c, 0), half * rows)
            k_copies[k] = go(remote(
                vbuf.at[t, at], vbuf.at[t, at],
                k_send.at[t, k], k_recv.at[t, k], (dom, core_peer)))
        for k in back:
            k_copies[k].wait_recv()
            loop(k * planes, (k + 1) * planes, phase(t), 1)
        for copy in sends:
            copy.wait_send()
        sweep(psi, u1)
        sweep(u1, u2)
        sweep(u2, u3)
        loop(0, GRID, last_sweep(keep if t < STEPS - 1 else finish))


def on_device(orbitals, occupations, core_density, ion_potential, neighbors, margin_widths):
    n = lax.axis_size("orb")
    doms = lax.axis_size("dom")
    r = GRID * GRID // (LANES * n)
    planes = GRID // CHUNKS
    rows = planes * r
    half, far = n // 2, n // 4
    total = GRID * GRID * GRID // LANES
    f32 = jnp.float32
    vmem, dma = pltpu.VMEM, pltpu.SemaphoreType.DMA
    state = vmem((GRID + 2, 8, 8, LANES), f32)
    T, K = STEPS, CHUNKS
    out, pot = pl.pallas_call(
        functools.partial(kernel, n, doms),
        out_shape=(
            jax.ShapeDtypeStruct((GRID, GRID, LANES), f32),
            jax.ShapeDtypeStruct((GRID, r * LANES), f32),
        ),
        in_specs=[
            pl.BlockSpec(memory_space=pltpu.VMEM),
            pl.BlockSpec(memory_space=pltpu.SMEM),
            pl.BlockSpec(memory_space=pltpu.SMEM),
            pl.BlockSpec(memory_space=pltpu.SMEM),
            pl.BlockSpec(memory_space=pl.ANY),
            pl.BlockSpec(memory_space=pl.ANY),
        ],
        out_specs=(pl.BlockSpec(memory_space=pltpu.VMEM), pl.BlockSpec(memory_space=pltpu.VMEM)),
        scratch_shapes=[
            state, state, state, state,
            vmem((GRID, r * LANES), f32), vmem((GRID, r * LANES), f32),
            vmem((total, LANES), f32),
            vmem((T, total, LANES), f32),
            vmem((T, K, half * rows, LANES), f32),
            vmem((T, K, far, rows, LANES), f32),
            vmem((T, K, far - 1, rows, LANES), f32),
            vmem((doms, 2, r, BUFFER, LANES), f32),
            vmem((doms, 2, r, BUFFER, LANES), f32),
            dma((2,)),
            dma((T, K)), dma((T, K)),
            dma((T, K, far)), dma((T, K, far)),
            dma((T, K, far - 1)), dma((T, K, far - 1)),
            dma((T, doms - 1)), dma((T, doms - 1)),
            dma((T, K, far - 1)), dma((T, K, far - 1)),
            dma((T, K, far)), dma((T, K, far)),
            dma((T, K)), dma((T, K)),
        ],
        compiler_params=pltpu.CompilerParams(
            collective_id=0, has_side_effects=True, vmem_limit_bytes=40 * 2**20
        ),
    )(orbitals[0, 0], occupations, neighbors, margin_widths, core_density[0], ion_potential[0])
    return out[None, None], pot[None]


def solution(mesh):
    return jax.shard_map(
        on_device,
        mesh=mesh,
        in_specs=(
            P("dom", "orb", None, None, None),
            P("dom", "orb"),
            P("dom", None, None),
            P("dom", None, None),
            P(),
            P(),
        ),
        out_specs=(P("dom", "orb", None, None, None), P("dom", None, "orb")),
        check_vma=False,
    )
```

time: 369 us -> 117 us (0.32); the launches traced: 362 us -> 116 us
  other arithmetic: 200 us -> 0 us
  Pallas kernels: 0 us -> 108 us
  waiting for transfers between devices: 87.3 us -> 0 us
  local copies, waits for them, and re-layouts: 45.9 us -> 7.34 us
  between operations: 20 us -> 1.3 us
  blocking collectives: 8.83 us -> 0 us
    mul x34 -> x0, other arithmetic: 135 us -> none  [the longest x16 107 us: kinetic(): applied = -0.5 * laplace(current)]
    pallas_call x0 -> x1, Pallas kernels: none -> 108 us  [on_device(): pl.pallas_call(functools.partial(kernel, n, doms), out_shape=(jax.ShapeDt...]
    reduce_scatter x2 -> x0, waiting for transfers between devices: 50.8 us -> none  [on_device(): lax.psum_scatter(terms, 'orb', scatter_dimension=1, tiled=True) + core_slab]
    all_gather x2 -> x0, waiting for transfers between devices: 36.4 us -> none  [on_device(): potential_full = lax.all_gather(slab_potential, 'orb', axis=1, tiled=True)]
    add x9 -> x0, other arithmetic: 21 us -> none  [the longest x3 11.4 us: kinetic(): result = result + current]
    another operation x16 -> x0, other arithmetic: 14.8 us -> none  [the longest x12 13.1 us: kinetic(): jnp.stack([factor * applied[..., 1, :], -factor * applied[..., 0, :]], ax...]
    add x2 -> x0, local copies, waits for them, and re-layouts: 13.5 us -> none  [kinetic(): result = result + current]
    reduce_sum x2 -> x0, other arithmetic: 12.8 us -> none  [on_device(): squares = jnp.sum(states * states, axis=3)]
  transfers between devices with their start and end apart: 4 -> 0, of which waited for: 4 -> 0; matrix products, arithmetic and copies ran while one was open for 24% -> 0% of each run, Pallas kernels for 0% -> 0%
where the time goes in v1:
time: 117 us; the launch traced here: 116 us
  Pallas kernels  108 us (92%)
  local copies, waits for them, and re-layouts  7.34 us (6%)
  between operations  1.3 us (1%)
    pallas_call x1, Pallas kernels, on_device(): pl.pallas_call(functools.partial(kernel, n, doms), out_shape=(jax.ShapeDt...  108 us
    unnamed x12, local copies, waits for them, and re-layouts  7.34 us

profile of v1, /device:TPU:0, one launch (start us, length us, event | category | flops | bytes accessed | tf_op | source)
XLA Modules:
  0.0 116.3 jit_solution(1167877829033880740)
XLA Ops:
  1.3 0.0 copy-start
  1.3 1.6 %copy-done = f32[1,1,64,64,128]{4,3,2,1,0:T(8,128)S(1)} copy-done((f32[1,1,64,64,128]{4,3,2,1,0:T(8,128)S(1)}, f32[1,1,64,64,128]{4,3,2,1,0:T(8,128)}, u32[]{:S(2)}) %copy-start) | copy-done | bytes 2097176
  2.9 0.0 copy-start.1
  2.9 1.2 %copy-done.1 = f32[1,64,4096]{2,1,0:T(8,128)S(1)} copy-done((f32[1,64,4096]{2,1,0:T(8,128)S(1)}, f32[1,64,4096]{2,1,0:T(8,128)}, u32[]{:S(2)}) %copy-start.1) | copy-done | bytes 1048600
  4.1 0.0 copy-start.2
  4.1 1.2 %copy-done.2 = f32[1,64,4096]{2,1,0:T(8,128)S(1)} copy-done((f32[1,64,4096]{2,1,0:T(8,128)S(1)}, f32[1,64,4096]{2,1,0:T(8,128)}, u32[]{:S(2)}) %copy-start.2) | copy-done | bytes 1048600
  5.3 0.0 copy-start.3
  5.3 0.7 copy-done.3
  6.0 0.0 copy-start.4
  6.0 0.7 copy-done.4
  6.7 107.7 %shard_map.77 = (f32[64,64,128]{2,1,0:T(8,128)S(1)}, f32[64,256]{1,0:T(8,128)S(1)}) custom-call(f32[64,64,128]{2,1,0:T(8,128)S(1)} %bitcast.5, f32[1,1]{1,0:T(1,128)S(6)} %copy.10.occ_ref, s32[2,2]{1,0:T(2,128)S(1)} %copy-done.3, s32[2,2]{1,0:T(2,128)S(1)} %copy-done.4, f32[64,4096]{1,0:T(8,128)S(1)} %bitcast.7, f32[64,4096]{1,0:T(8,128)S(1)} %bitcast.8), custom_call_target="tpu_custom_call" | custom-call | tf_op jit(solution)/shard_map/pallas_call | solution.py:342
  114.3 1.3 %copy.11 = f32[1,1,64,64,128]{4,3,2,1,0:T(8,128)} copy(f32[1,1,64,64,128]{4,3,2,1,0:T(8,128)S(1)} %bitcast.6) | data formatting | bytes 4194304
  115.7 0.6 copy.12
Async XLA Ops:
  1.3 1.6 %copy-start = (f32[1,1,64,64,128]{4,3,2,1,0:T(8,128)S(1)}, f32[1,1,64,64,128]{4,3,2,1,0:T(8,128)}, u32[]{:S(2)}) copy-start(f32[1,1,64,64,128]{4,3,2,1,0:T(8,128)} %param.6) | copy-start | bytes 6291460
  2.9 1.2 %copy-start.1 = (f32[1,64,4096]{2,1,0:T(8,128)S(1)}, f32[1,64,4096]{2,1,0:T(8,128)}, u32[]{:S(2)}) copy-start(f32[1,64,4096]{2,1,0:T(8,128)} %param.8) | copy-start | bytes 3145732
  4.1 1.2 %copy-start.2 = (f32[1,64,4096]{2,1,0:T(8,128)S(1)}, f32[1,64,4096]{2,1,0:T(8,128)}, u32[]{:S(2)}) copy-start(f32[1,64,4096]{2,1,0:T(8,128)} %param.9) | copy-start | bytes 3145732
  5.3 0.7 copy-start.3
  6.0 0.7 copy-start.4

commit v2 on v1

--- a/solution.py
+++ b/solution.py
@@ -190,16 +190,9 @@
             return copy
 
         a_copies = {}
-        for k in order:
-            loop(k * planes, (k + 1) * planes, density_again if t else load_in)
-            if t == 0 and k == order[0]:
-                pl.semaphore_wait(barrier, len(peers))
-            a_copies[k] = go(remote(
-                dens.at[pl.ds(rows_at(k, 1 - c, 0), half * rows)],
-                recv_a.at[t, k], a_send.at[t, k], a_recv.at[t, k], (dom, core_peer)))
-        sweep(psi, u1)
         b_copies = {}
-        for k in order:
+
+        def start_x(k):
             a_copies[k].wait_recv()
             for mm in range(half):
                 at = pl.ds(rows_at(k, c, mm), rows)
@@ -209,7 +202,18 @@
                 b_copies[k].append(go(remote(
                     dens.at[pl.ds(rows_at(k, c, 2 * i + 1 - b), rows)],
                     recv_b.at[t, k, i], b_send.at[t, k, i], b_recv.at[t, k, i], (dom, x_peer))))
-        sweep(u1, u2)
+
+        for place, k in enumerate(order):
+            loop(k * planes, (k + 1) * planes, density_again if t else load_in)
+            if t == 0 and k == order[0]:
+                pl.semaphore_wait(barrier, len(peers))
+            a_copies[k] = go(remote(
+                dens.at[pl.ds(rows_at(k, 1 - c, 0), half * rows)],
+                recv_a.at[t, k], a_send.at[t, k], a_recv.at[t, k], (dom, core_peer)))
+            if place:
+                start_x(order[place - 1])
+        start_x(order[-1])
+        sweep(psi, u1)
         c_copies = {}
         for k in order:
             for i in range(far):
@@ -222,6 +226,7 @@
                 c_copies[k].append(go(remote(
                     dens.at[pl.ds(rows_at(k, c, 2 * other + b), rows)],
                     recv_c.at[t, k, i - 1], c_send.at[t, k, i - 1], c_recv.at[t, k, i - 1], (dom, peer))))
+        sweep(u1, u2)
         sweep(u2, u3)
         if t == 0:
             for load in loads:
@@ -318,7 +323,7 @@
                 k_send.at[t, k], k_recv.at[t, k], (dom, core_peer)))
         for k in back:
             k_copies[k].wait_recv()
-            loop(k * planes, (k + 1) * planes, phase(t), 1)
+            loop(k * planes, (k + 1) * planes, phase(t), 2)
         for copy in sends:
             copy.wait_send()
         sweep(psi, u1)

time: 117 us -> 112 us (0.957)
  Pallas kernels: 108 us -> 103 us
    pallas_call x1, Pallas kernels: 108 us -> 103 us  [on_device(): pl.pallas_call(functools.partial(kernel, n, doms), out_shape=(jax.ShapeDt...]
where the time goes in v2:
time: 112 us
  Pallas kernels  103 us (92%)
  local copies, waits for them, and re-layouts  7.34 us (7%)
  between operations  1.3 us (1%)
    pallas_call x1, Pallas kernels, on_device(): pl.pallas_call(functools.partial(kernel, n, doms), out_shape=(jax.ShapeDt...  103 us
    unnamed x12, local copies, waits for them, and re-layouts  7.34 us

profile of v2, /device:TPU:0, one launch (start us, length us, event | category | flops | bytes accessed | tf_op | source)
XLA Modules:
  0.0 112.0 jit_solution(11170587414337012016)
XLA Ops:
  1.3 0.0 copy-start
  1.3 1.6 %copy-done = f32[1,1,64,64,128]{4,3,2,1,0:T(8,128)S(1)} copy-done((f32[1,1,64,64,128]{4,3,2,1,0:T(8,128)S(1)}, f32[1,1,64,64,128]{4,3,2,1,0:T(8,128)}, u32[]{:S(2)}) %copy-start) | copy-done | bytes 2097176
  2.9 0.0 copy-start.1
  2.9 1.2 %copy-done.1 = f32[1,64,4096]{2,1,0:T(8,128)S(1)} copy-done((f32[1,64,4096]{2,1,0:T(8,128)S(1)}, f32[1,64,4096]{2,1,0:T(8,128)}, u32[]{:S(2)}) %copy-start.1) | copy-done | bytes 1048600
  4.1 0.0 copy-start.2
  4.1 1.2 %copy-done.2 = f32[1,64,4096]{2,1,0:T(8,128)S(1)} copy-done((f32[1,64,4096]{2,1,0:T(8,128)S(1)}, f32[1,64,4096]{2,1,0:T(8,128)}, u32[]{:S(2)}) %copy-start.2) | copy-done | bytes 1048600
  5.3 0.0 copy-start.3
  5.3 0.7 copy-done.3
  6.0 0.0 copy-start.4
  6.0 0.7 copy-done.4
  6.7 103.4 %shard_map.77 = (f32[64,64,128]{2,1,0:T(8,128)S(1)}, f32[64,256]{1,0:T(8,128)S(1)}) custom-call(f32[64,64,128]{2,1,0:T(8,128)S(1)} %bitcast.5, f32[1,1]{1,0:T(1,128)S(6)} %copy.10.occ_ref, s32[2,2]{1,0:T(2,128)S(1)} %copy-done.3, s32[2,2]{1,0:T(2,128)S(1)} %copy-done.4, f32[64,4096]{1,0:T(8,128)S(1)} %bitcast.7, f32[64,4096]{1,0:T(8,128)S(1)} %bitcast.8), custom_call_target="tpu_custom_call" | custom-call | tf_op jit(solution)/shard_map/pallas_call | solution.py:347
  110.1 1.3 %copy.11 = f32[1,1,64,64,128]{4,3,2,1,0:T(8,128)} copy(f32[1,1,64,64,128]{4,3,2,1,0:T(8,128)S(1)} %bitcast.6) | data formatting | bytes 4194304
  111.4 0.6 copy.12
Async XLA Ops:
  1.3 1.6 %copy-start = (f32[1,1,64,64,128]{4,3,2,1,0:T(8,128)S(1)}, f32[1,1,64,64,128]{4,3,2,1,0:T(8,128)}, u32[]{:S(2)}) copy-start(f32[1,1,64,64,128]{4,3,2,1,0:T(8,128)} %param.6) | copy-start | bytes 6291460
  2.9 1.2 %copy-start.1 = (f32[1,64,4096]{2,1,0:T(8,128)S(1)}, f32[1,64,4096]{2,1,0:T(8,128)}, u32[]{:S(2)}) copy-start(f32[1,64,4096]{2,1,0:T(8,128)} %param.8) | copy-start | bytes 3145732
  4.1 1.2 %copy-start.2 = (f32[1,64,4096]{2,1,0:T(8,128)S(1)}, f32[1,64,4096]{2,1,0:T(8,128)}, u32[]{:S(2)}) copy-start(f32[1,64,4096]{2,1,0:T(8,128)} %param.9) | copy-start | bytes 3145732
  5.3 0.7 copy-start.3
  6.0 0.7 copy-start.4
